TPU v7x, 32 devices: a whole 2x2x4 slice. The times are simulated.
32 devices in a mesh: dp: 4 (over y, x), fsdp: 8 (over z, core).
Axes of the slice: x: 2, y: 2, z: 4, core: 2. Of those that a mesh axis runs over, the one named last changes fastest.
Arguments:
- full_input: bfloat16 [32, 256, 1152], P(('dp', 'fsdp')), may hold values from -6 to 6
- masked_input: bfloat16 [32, 256, 1152], P(('dp', 'fsdp')), may hold values from -6 to 6
- keep_index: int32 [32, 128], P(('dp', 'fsdp')), may hold values from 0 to 255, as said below
- cond_full: bfloat16 [32, 1152], P(('dp', 'fsdp')), may hold values from -6 to 6
- cond_masked: bfloat16 [32, 1152], P(('dp', 'fsdp')), may hold values from -6 to 6
- w_ada: bfloat16 [1152, 6912], P('dp', 'fsdp'), may hold values from -0.1875 to 0.1875
- b_ada: bfloat16 [6912], P('fsdp'), may hold values from -4 to 4
- w_qkv: bfloat16 [1152, 3456], P('dp', 'fsdp'), may hold values from -0.1875 to 0.1875
- b_q: bfloat16 [1152], P('fsdp'), may hold values from -6 to 6
- b_v: bfloat16 [1152], P('fsdp'), may hold values from -6 to 6
- w_out: bfloat16 [1152, 1152], P('dp', 'fsdp'), may hold values from -0.75 to 0.75
- b_out: bfloat16 [1152], P('fsdp'), may hold values from -4 to 4
- w_fc1: bfloat16 [1152, 4608], P('dp', 'fsdp'), may hold values from -0.1875 to 0.1875
- b_fc1: bfloat16 [4608], P('fsdp'), may hold values from -4 to 4
- w_fc2: bfloat16 [4608, 1152], P('dp', 'fsdp'), may hold values from -0.09375 to 0.09375
- b_fc2: bfloat16 [1152], P('fsdp'), may hold values from -4 to 4
- cot_full: bfloat16 [32, 256, 1152], P(('dp', 'fsdp')), may hold values from -6 to 6
- cot_masked: bfloat16 [32, 128, 1152], P(('dp', 'fsdp')), may hold values from -6 to 6
Outputs:
- out_full: bfloat16 [32, 256, 1152], P(('dp', 'fsdp'))
- out_masked: bfloat16 [32, 128, 1152], P(('dp', 'fsdp'))
- grad_full: float32 [32, 256, 1152], P(('dp', 'fsdp'))
- grad_masked: float32 [32, 256, 1152], P(('dp', 'fsdp'))
- grad_cond_full: float32 [32, 1152], P(('dp', 'fsdp'))
- grad_cond_masked: float32 [32, 1152], P(('dp', 'fsdp'))
- grad_w_ada: float32 [1152, 6912], P('dp', 'fsdp')
- grad_b_ada: float32 [6912], P('fsdp')
- grad_w_qkv: float32 [1152, 3456], P('dp', 'fsdp')
- grad_b_q: float32 [1152], P('fsdp')
- grad_b_v: float32 [1152], P('fsdp')
- grad_w_out: float32 [1152, 1152], P('dp', 'fsdp')
- grad_b_out: float32 [1152], P('fsdp')
- grad_w_fc1: float32 [1152, 4608], P('dp', 'fsdp')
- grad_b_fc1: float32 [4608], P('fsdp')
- grad_w_fc2: float32 [4608, 1152], P('dp', 'fsdp')
- grad_b_fc2: float32 [1152], P('fsdp')
Inputs may be any that keep to these rules, and one draw needn't show every extreme that they name: `keep_index`: each row holds 128 distinct positions of one image in increasing order.
All inputs are finite; a program needn't handle non-finite values.
Results may differ from a plain program's by a relative error of at most 0.02.
Values may be sent and summed in bfloat16 or wider, within the bound.
A program may use at most 256 MiB of HBM per device.

v0:
```python
import math

import jax
import jax.numpy as jnp
from jax import lax
from jax.sharding import PartitionSpec as P

HEAD_DIM = 72


def layer_stats(values):
    centered = values - jnp.mean(values, axis=-1, keepdims=True)
    inverse = lax.rsqrt(jnp.mean(centered * centered, axis=-1, keepdims=True) + 1e-06)
    return (centered * inverse, inverse)


def layer_back(upstream, normed, inverse):
    return inverse * (
        upstream
        - jnp.mean(upstream, axis=-1, keepdims=True)
        - normed * jnp.mean(upstream * normed, axis=-1, keepdims=True)
    )


def gelu_tanh(values):
    return jax.nn.gelu(values, approximate=True)


def expand_mods(piece, full_length, kept_length):
    head_part = jnp.broadcast_to(piece[:, 0:1], (piece.shape[0], full_length, piece.shape[2]))
    tail_part = jnp.broadcast_to(piece[:, 1:2], (piece.shape[0], kept_length, piece.shape[2]))
    return jnp.concatenate([head_part, tail_part], axis=1)


def image_sums(values, full_length):
    return jnp.stack(
        [jnp.sum(values[:, :full_length], axis=1), jnp.sum(values[:, full_length:], axis=1)], axis=1
    )


def forward_pass(tokens, mods, weights, biases, full_length):
    images, length, features = tokens.shape
    head_count = features // HEAD_DIM
    pieces = [
        expand_mods(
            mods[:, :, column * features : (column + 1) * features],
            full_length,
            length - full_length,
        )
        for column in range(6)
    ]
    norm_one, inverse_one = layer_stats(tokens)
    hidden_one = (norm_one * (1.0 + pieces[1]) + pieces[0]).astype(jnp.bfloat16)
    bias_all = jnp.concatenate([biases[1], jnp.zeros((features,), jnp.bfloat16), biases[2]]).astype(
        jnp.float32
    )
    projected = (
        jnp.einsum("itd,de->ite", hidden_one, weights[1], preferred_element_type=jnp.float32)
        + bias_all
    )
    projected = projected.astype(jnp.bfloat16).reshape(images, length, 3, head_count, HEAD_DIM)
    query_rows = projected[:, :, 0]
    key_rows = projected[:, :, 1]
    value_rows = projected[:, :, 2]
    scale_factor = 1.0 / math.sqrt(HEAD_DIM)
    scores = (
        jnp.einsum("iqhc,ikhc->ihqk", query_rows, key_rows, preferred_element_type=jnp.float32)
        * scale_factor
    )
    marker = jnp.arange(length) >= full_length
    same_image = marker[:, None] == marker[None, :]
    scores = jnp.where(same_image, scores, -1e30)
    row_max = jnp.max(scores, axis=-1, keepdims=True)
    exponent = jnp.exp(scores - row_max)
    attention = exponent / jnp.sum(exponent, axis=-1, keepdims=True)
    attention_low = attention.astype(jnp.bfloat16)
    mixed = jnp.einsum(
        "ihqk,ikhc->iqhc", attention_low, value_rows, preferred_element_type=jnp.float32
    )
    mixed = mixed.astype(jnp.bfloat16).reshape(images, length, features)
    attn_out = jnp.einsum(
        "itd,de->ite", mixed, weights[2], preferred_element_type=jnp.float32
    ) + biases[3].astype(jnp.float32)
    residual = tokens + pieces[2] * attn_out
    norm_two, inverse_two = layer_stats(residual)
    hidden_two = (norm_two * (1.0 + pieces[4]) + pieces[3]).astype(jnp.bfloat16)
    upper = jnp.einsum(
        "itd,df->itf", hidden_two, weights[3], preferred_element_type=jnp.float32
    ) + biases[4].astype(jnp.float32)
    activated = gelu_tanh(upper).astype(jnp.bfloat16)
    branch = jnp.einsum(
        "itf,fd->itd", activated, weights[4], preferred_element_type=jnp.float32
    ) + biases[5].astype(jnp.float32)
    result = residual + pieces[5] * branch
    return (
        result,
        pieces,
        norm_one,
        inverse_one,
        hidden_one,
        query_rows,
        key_rows,
        value_rows,
        attention,
        attention_low,
        mixed,
        attn_out,
        norm_two,
        inverse_two,
        hidden_two,
        upper,
        activated,
        branch,
    )


def on_device(
    full_input,
    masked_input,
    keep_index,
    cond_full,
    cond_masked,
    w_ada,
    b_ada,
    w_qkv,
    b_q,
    b_v,
    w_out,
    b_out,
    w_fc1,
    b_fc1,
    w_fc2,
    b_fc2,
    cot_full,
    cot_masked,
):
    row_blocks = (
        lax.all_gather(w_ada, "dp", axis=0, tiled=True),
        lax.all_gather(w_qkv, "dp", axis=0, tiled=True),
        lax.all_gather(w_out, "dp", axis=0, tiled=True),
        lax.all_gather(w_fc1, "dp", axis=0, tiled=True),
        lax.all_gather(w_fc2, "dp", axis=0, tiled=True),
    )
    gathered = (
        lax.all_gather(row_blocks[0], "fsdp", axis=1, tiled=True),
        lax.all_gather(row_blocks[1], "fsdp", axis=1, tiled=True),
        lax.all_gather(row_blocks[2], "fsdp", axis=1, tiled=True),
        lax.all_gather(row_blocks[3], "fsdp", axis=1, tiled=True),
        lax.all_gather(row_blocks[4], "fsdp", axis=1, tiled=True),
        lax.all_gather(b_ada, "fsdp", axis=0, tiled=True),
        lax.all_gather(b_q, "fsdp", axis=0, tiled=True),
        lax.all_gather(b_v, "fsdp", axis=0, tiled=True),
        lax.all_gather(b_out, "fsdp", axis=0, tiled=True),
        lax.all_gather(b_fc1, "fsdp", axis=0, tiled=True),
        lax.all_gather(b_fc2, "fsdp", axis=0, tiled=True),
    )
    weights = gathered[:5]
    biases = gathered[5:]
    full_length = full_input.shape[1]
    images = full_input.shape[0]
    features = full_input.shape[2]
    picked = jnp.take_along_axis(masked_input, keep_index[:, :, None], axis=1)
    tokens = jnp.concatenate([full_input, picked], axis=1).astype(jnp.float32)
    conds = jnp.stack([cond_full, cond_masked], axis=1).astype(jnp.float32)
    silu_low = jax.nn.silu(conds).astype(jnp.bfloat16)
    mods = jnp.einsum(
        "ijd,de->ije", silu_low, weights[0], preferred_element_type=jnp.float32
    ) + biases[0].astype(jnp.float32)
    result = forward_pass(tokens, mods, weights, biases, full_length)[0]
    again_rows = (
        lax.all_gather(w_ada, "dp", axis=0, tiled=True),
        lax.all_gather(w_qkv, "dp", axis=0, tiled=True),
        lax.all_gather(w_out, "dp", axis=0, tiled=True),
        lax.all_gather(w_fc1, "dp", axis=0, tiled=True),
        lax.all_gather(w_fc2, "dp", axis=0, tiled=True),
    )
    again = (
        lax.all_gather(again_rows[0], "fsdp", axis=1, tiled=True),
        lax.all_gather(again_rows[1], "fsdp", axis=1, tiled=True),
        lax.all_gather(again_rows[2], "fsdp", axis=1, tiled=True),
        lax.all_gather(again_rows[3], "fsdp", axis=1, tiled=True),
        lax.all_gather(again_rows[4], "fsdp", axis=1, tiled=True),
        lax.all_gather(b_ada, "fsdp", axis=0, tiled=True),
        lax.all_gather(b_q, "fsdp", axis=0, tiled=True),
        lax.all_gather(b_v, "fsdp", axis=0, tiled=True),
        lax.all_gather(b_out, "fsdp", axis=0, tiled=True),
        lax.all_gather(b_fc1, "fsdp", axis=0, tiled=True),
        lax.all_gather(b_fc2, "fsdp", axis=0, tiled=True),
    )
    weights = again[:5]
    biases = again[5:]
    (
        recomputed,
        pieces,
        norm_one,
        inverse_one,
        hidden_one,
        query_rows,
        key_rows,
        value_rows,
        attention,
        attention_low,
        mixed,
        attn_out,
        norm_two,
        inverse_two,
        hidden_two,
        upper,
        activated,
        branch,
    ) = forward_pass(tokens, mods, weights, biases, full_length)
    length = tokens.shape[1]
    head_count = features // HEAD_DIM
    scale_factor = 1.0 / math.sqrt(HEAD_DIM)
    grad_result = jnp.concatenate([cot_full, cot_masked], axis=1).astype(jnp.float32)
    grad_gate_two = image_sums(grad_result * branch, full_length)
    grad_branch = (pieces[5] * grad_result).astype(jnp.bfloat16)
    grad_b_fc2 = jnp.sum(grad_branch.astype(jnp.float32), axis=(0, 1))
    grad_w_fc2 = jnp.einsum(
        "itf,itd->fd", activated, grad_branch, preferred_element_type=jnp.float32
    )
    grad_act = jnp.einsum(
        "itd,fd->itf", grad_branch, weights[4], preferred_element_type=jnp.float32
    )
    grad_upper = jax.vjp(gelu_tanh, upper)[1](grad_act)[0].astype(jnp.bfloat16)
    grad_b_fc1 = jnp.sum(grad_upper.astype(jnp.float32), axis=(0, 1))
    grad_w_fc1 = jnp.einsum(
        "itd,itf->df", hidden_two, grad_upper, preferred_element_type=jnp.float32
    )
    grad_hidden_two = jnp.einsum(
        "itf,df->itd", grad_upper, weights[3], preferred_element_type=jnp.float32
    )
    grad_scale_two = image_sums(grad_hidden_two * norm_two, full_length)
    grad_shift_two = image_sums(grad_hidden_two, full_length)
    grad_residual = grad_result + layer_back(
        grad_hidden_two * (1.0 + pieces[4]), norm_two, inverse_two
    )
    grad_gate_one = image_sums(grad_residual * attn_out, full_length)
    grad_attn = (pieces[2] * grad_residual).astype(jnp.bfloat16)
    grad_b_out = jnp.sum(grad_attn.astype(jnp.float32), axis=(0, 1))
    grad_w_out = jnp.einsum("itd,ite->de", mixed, grad_attn, preferred_element_type=jnp.float32)
    grad_mixed = jnp.einsum(
        "ite,de->itd", grad_attn, weights[2], preferred_element_type=jnp.float32
    )
    grad_mixed = grad_mixed.astype(jnp.bfloat16).reshape(images, length, head_count, HEAD_DIM)
    grad_attention = jnp.einsum(
        "iqhc,ikhc->ihqk", grad_mixed, value_rows, preferred_element_type=jnp.float32
    )
    grad_values = jnp.einsum(
        "ihqk,iqhc->ikhc", attention_low, grad_mixed, preferred_element_type=jnp.float32
    )
    grad_scores = attention * (
        grad_attention - jnp.sum(attention * grad_attention, axis=-1, keepdims=True)
    )
    grad_scores = grad_scores.astype(jnp.bfloat16)
    grad_queries = (
        jnp.einsum("ihqk,ikhc->iqhc", grad_scores, key_rows, preferred_element_type=jnp.float32)
        * scale_factor
    )
    grad_keys = (
        jnp.einsum("ihqk,iqhc->ikhc", grad_scores, query_rows, preferred_element_type=jnp.float32)
        * scale_factor
    )
    grad_projected = jnp.stack([grad_queries, grad_keys, grad_values], axis=2)
    grad_projected = grad_projected.reshape(images, length, 3 * features).astype(jnp.bfloat16)
    grad_b_q = jnp.sum(grad_projected[:, :, :features].astype(jnp.float32), axis=(0, 1))
    grad_b_v = jnp.sum(grad_projected[:, :, 2 * features :].astype(jnp.float32), axis=(0, 1))
    grad_w_qkv = jnp.einsum(
        "itd,ite->de", hidden_one, grad_projected, preferred_element_type=jnp.float32
    )
    grad_hidden_one = jnp.einsum(
        "ite,de->itd", grad_projected, weights[1], preferred_element_type=jnp.float32
    )
    grad_scale_one = image_sums(grad_hidden_one * norm_one, full_length)
    grad_shift_one = image_sums(grad_hidden_one, full_length)
    grad_tokens = grad_residual + layer_back(
        grad_hidden_one * (1.0 + pieces[1]), norm_one, inverse_one
    )
    grad_mods = jnp.concatenate(
        [
            grad_shift_one,
            grad_scale_one,
            grad_gate_one,
            grad_shift_two,
            grad_scale_two,
            grad_gate_two,
        ],
        axis=-1,
    ).astype(jnp.bfloat16)
    grad_b_ada = jnp.sum(grad_mods.astype(jnp.float32), axis=(0, 1))
    grad_w_ada = jnp.einsum("ijd,ije->de", silu_low, grad_mods, preferred_element_type=jnp.float32)
    grad_silu = jnp.einsum("ije,de->ijd", grad_mods, weights[0], preferred_element_type=jnp.float32)
    grad_cond = jax.vjp(jax.nn.silu, conds)[1](grad_silu)[0]
    image_rows = jnp.arange(images)[:, None]
    grad_masked = (
        jnp.zeros((images, full_length, features), jnp.float32)
        .at[image_rows, keep_index]
        .set(grad_tokens[:, full_length:])
    )
    inner = (
        lax.psum_scatter(
            grad_w_ada.astype(jnp.bfloat16), "dp", scatter_dimension=0, tiled=True
        ).astype(jnp.float32),
        lax.psum_scatter(
            grad_w_qkv.astype(jnp.bfloat16), "dp", scatter_dimension=0, tiled=True
        ).astype(jnp.float32),
        lax.psum_scatter(
            grad_w_out.astype(jnp.bfloat16), "dp", scatter_dimension=0, tiled=True
        ).astype(jnp.float32),
        lax.psum_scatter(
            grad_w_fc1.astype(jnp.bfloat16), "dp", scatter_dimension=0, tiled=True
        ).astype(jnp.float32),
        lax.psum_scatter(
            grad_w_fc2.astype(jnp.bfloat16), "dp", scatter_dimension=0, tiled=True
        ).astype(jnp.float32),
    )
    totals = (
        lax.psum(grad_b_ada.astype(jnp.bfloat16), "dp").astype(jnp.float32),
        lax.psum(grad_b_q.astype(jnp.bfloat16), "dp").astype(jnp.float32),
        lax.psum(grad_b_v.astype(jnp.bfloat16), "dp").astype(jnp.float32),
        lax.psum(grad_b_out.astype(jnp.bfloat16), "dp").astype(jnp.float32),
        lax.psum(grad_b_fc1.astype(jnp.bfloat16), "dp").astype(jnp.float32),
        lax.psum(grad_b_fc2.astype(jnp.bfloat16), "dp").astype(jnp.float32),
    )
    summed = (
        lax.psum_scatter(
            inner[0].astype(jnp.bfloat16), "fsdp", scatter_dimension=1, tiled=True
        ).astype(jnp.float32),
        lax.psum_scatter(
            inner[1].astype(jnp.bfloat16), "fsdp", scatter_dimension=1, tiled=True
        ).astype(jnp.float32),
        lax.psum_scatter(
            inner[2].astype(jnp.bfloat16), "fsdp", scatter_dimension=1, tiled=True
        ).astype(jnp.float32),
        lax.psum_scatter(
            inner[3].astype(jnp.bfloat16), "fsdp", scatter_dimension=1, tiled=True
        ).astype(jnp.float32),
        lax.psum_scatter(
            inner[4].astype(jnp.bfloat16), "fsdp", scatter_dimension=1, tiled=True
        ).astype(jnp.float32),
        lax.psum_scatter(
            totals[0].astype(jnp.bfloat16), "fsdp", scatter_dimension=0, tiled=True
        ).astype(jnp.float32),
        lax.psum_scatter(
            totals[1].astype(jnp.bfloat16), "fsdp", scatter_dimension=0, tiled=True
        ).astype(jnp.float32),
        lax.psum_scatter(
            totals[2].astype(jnp.bfloat16), "fsdp", scatter_dimension=0, tiled=True
        ).astype(jnp.float32),
        lax.psum_scatter(
            totals[3].astype(jnp.bfloat16), "fsdp", scatter_dimension=0, tiled=True
        ).astype(jnp.float32),
        lax.psum_scatter(
            totals[4].astype(jnp.bfloat16), "fsdp", scatter_dimension=0, tiled=True
        ).astype(jnp.float32),
        lax.psum_scatter(
            totals[5].astype(jnp.bfloat16), "fsdp", scatter_dimension=0, tiled=True
        ).astype(jnp.float32),
    )
    matrices = summed[:5]
    vectors = summed[5:]
    return (
        result[:, :full_length].astype(jnp.bfloat16),
        result[:, full_length:].astype(jnp.bfloat16),
        grad_tokens[:, :full_length],
        grad_masked,
        grad_cond[:, 0],
        grad_cond[:, 1],
        matrices[0],
        vectors[0],
        matrices[1],
        vectors[1],
        vectors[2],
        matrices[2],
        vectors[3],
        matrices[3],
        vectors[4],
        matrices[4],
        vectors[5],
    )


def solution(mesh):
    return jax.shard_map(
        on_device,
        mesh=mesh,
        in_specs=(
            P(("dp", "fsdp"), None, None),
            P(("dp", "fsdp"), None, None),
            P(("dp", "fsdp"), None),
            P(("dp", "fsdp"), None),
            P(("dp", "fsdp"), None),
            P("dp", "fsdp"),
            P("fsdp"),
            P("dp", "fsdp"),
            P("fsdp"),
            P("fsdp"),
            P("dp", "fsdp"),
            P("fsdp"),
            P("dp", "fsdp"),
            P("fsdp"),
            P("dp", "fsdp"),
            P("fsdp"),
            P(("dp", "fsdp"), None, None),
            P(("dp", "fsdp"), None, None),
        ),
        out_specs=(
            P(("dp", "fsdp"), None, None),
            P(("dp", "fsdp"), None, None),
            P(("dp", "fsdp"), None, None),
            P(("dp", "fsdp"), None, None),
            P(("dp", "fsdp"), None),
            P(("dp", "fsdp"), None),
            P("dp", "fsdp"),
            P("fsdp"),
            P("dp", "fsdp"),
            P("fsdp"),
            P("fsdp"),
            P("dp", "fsdp"),
            P("fsdp"),
            P("dp", "fsdp"),
            P("fsdp"),
            P("dp", "fsdp"),
            P("fsdp"),
        ),
        check_vma=False,
    )
```

profile of v0, /device:TPU:0, one launch (start us, length us, event | category | flops | bytes accessed | tf_op | source)
XLA Modules:
  0.0 1353.5 jit_solution(14359141284881043124)
XLA Ops:
  9.5 38.2 %all-gather.10.cloned.1.call-done = bf16[1152,864]{1,0:T(8,128)(2,1)} async-done(((bf16[288,864]{1,0:T(8,128)(2,1)}), bf16[1152,864]{1,0:T(8,128)(2,1)}) %all-gather.10.cloned.1.call-update) | async-done | bytes 1990672 | tf_op jit(solution)/shard_map/all_gather | solution.py:138
  52.7 17.4 %all_gather.66 = bf16[1152,432]{1,0:T(8,128)(2,1)S(1)} all-gather(bf16[288,432]{1,0:T(8,128)(2,1)S(1)} %copy-done.41), channel_id=1, replica_groups=mesh['dp'=4,'fsdp'=8] {'dp'}, dimensions={0}, use_global_device_ids=true | all-gather | bytes 1244160 | tf_op jit(solution)/shard_map/all_gather | solution.py:139
  71.7 13.9 %all-gather = bf16[4,288,144]{1,2,0:T(8,128)(2,1)S(1)} all-gather(bf16[1,288,144]{1,2,0:T(8,128)(2,1)S(1)} %bitcast.199), channel_id=1, replica_groups=mesh['dp'=4,'fsdp'=8] {'dp'}, dimensions={0}, use_global_device_ids=true | all-gather | bytes 414720 | tf_op jit(solution)/shard_map/all_gather | solution.py:140
  89.6 27.9 %all-gather.22.cloned.1.call-done = bf16[4608,144]{0,1:T(8,128)(2,1)} async-done(((bf16[1152,144]{0,1:T(8,128)(2,1)}), bf16[4608,144]{0,1:T(8,128)(2,1)}) %all-gather.22.cloned.1.call-update) | async-done | bytes 1327120 | tf_op jit(solution)/shard_map/all_gather | solution.py:142
  121.7 30.5 %all-reduce.14 = (bf16[1152]{0:T(1024)(128)(2,1)S(1)}, bf16[1152]{0:T(1024)(128)(2,1)S(1)}, bf16[6912]{0:T(1024)(128)(2,1)S(1)}, bf16[1152]{0:T(1024)(128)(2,1)S...) all-reduce(bf16[1152]{0:T(1024)(128)(2,1)S(1)} %dynamic-update-slic, ...), channel_id=1, replica_groups=mesh['dp'=4,'fsdp'=8] {'fsdp'}, use_global_device_ids=true, to_apply=%add.3 | all-reduce | flops 16128 | bytes 64512
  156.8 107.1 %all-gather.12.cloned.1.call-done = bf16[1152,6912]{0,1:T(8,128)(2,1)} async-done(((bf16[1152,864]{0,1:T(8,128)(2,1)}), bf16[1152,6912]{0,1:T(8,128)(2,1)}) %all-gather.12.cloned.1.call-update) | async-done | bytes 15925264 | tf_op jit(solution)/shard_map/all_gather | solution.py:145
  263.9 9.7 fusion.1
  274.4 68.4 %all-gather.14.cloned.1.call-done = bf16[1152,3456]{0,1:T(8,128)(2,1)} async-done(((bf16[1152,432]{0,1:T(8,128)(2,1)}), bf16[1152,3456]{0,1:T(8,128)(2,1)}) %all-gather.14.cloned.1.call-update) | async-done | bytes 7962640 | tf_op jit(solution)/shard_map/all_gather | solution.py:146
  344.1 10.4 fusion.10
  370.5 7.2 all-gather.16.cloned.1.call-done
  385.1 93.7 %all-gather.20.cloned.1.call-done = bf16[1152,4608]{0,1:T(8,128)(2,1)} async-done(((bf16[1152,576]{0,1:T(8,128)(2,1)}), bf16[1152,4608]{0,1:T(8,128)(2,1)}) %all-gather.20.cloned.1.call-update) | async-done | bytes 10616848 | tf_op jit(solution)/shard_map/all_gather | solution.py:148
  482.7 15.0 %convolution_add_fusion.1 = f32[384,4608]{1,0:T(8,128)} fusion(bf16[1152,4608]{0,1:T(8,128)(2,1)} %all-gather.20.cloned.1.call-done, f32[4608]{0:T(1024)S(1)} %copy-done.93, f32[128,1152]{1,0:T(8,128)S(1)} %broadcast_in_dim.103, f32[256,1152]{1,0:T(8,128)S(1)} %broadcast_in_dim.101, f32[128,1152]{1,0:T(8,128)S(1)} %broadcast_in_dim.107, ...), kind=kOutput, calls=%fused_computation.17 | convolution fusion | flops 4082171904 | bytes 23024640 | tf_op jit(solution)/shard_map/itd,df->itf/dot_general | solution.py:87
  497.7 81.7 %all-gather.24.cloned.1.call-done = bf16[4608,1152]{0,1:T(8,128)(2,1)} async-done(((bf16[4608,144]{0,1:T(8,128)(2,1)}), bf16[4608,1152]{0,1:T(8,128)(2,1)}) %all-gather.24.cloned.1.call-update) | async-done | bytes 10616848 | tf_op jit(solution)/shard_map/all_gather | solution.py:149
  580.7 12.9 fusion.114
  601.3 15.9 %fusion.34 = (f32[1,384,1152]{2,1,0:T(8,128)}, bf16[1,384,1152]{2,1,0:T(8,128)(2,1)}, f32[1,384,1152]{2,1,0:T(8,128)}, f32[384]{0:T(512)}, f32[384]{0:T(512)}) fusion(bf16[128,1152]{1,0:T(8,128)(2,1)} %bitcast.187, bf16[256,1152]{1,0:T(8,128)(2,1)} %bitcast.183, f32[384,1152]{1,0:T(8,128)S(1)} %get-tuple-element.141, f32[128,1152]{1,0:T(8,128)} %copy-done.37, ...), kind=kOutput, calls=%fused_computation.63 | convolution fusion | flops 4101192704 | bytes 30091776 | tf_op jit(solution)/shard_map/itf,fd->itd/dot_general | solution.py:91
  633.3 9.0 multiply_reduce_fusion
  642.4 11.0 multiply_convert_fusion
  668.7 7.6 convolution_convert_fusion.3
  677.6 11.1 convolution_convert_fusion.2
  690.5 11.3 convolution_convert_fusion.1
  703.7 8.3 fusion.74
  719.8 7.8 convolution_convert_fusion
  730.2 28.2 %reduce-scatter.23.cloned.1.call-done = bf16[288,3456]{1,0:T(8,128)(2,1)} async-done(((bf16[1152,3456]{1,0:T(8,128)(2,1)}), bf16[288,3456]{1,0:T(8,128)(2,1)}) %reduce-scatter.23.cloned.1.call-update) | async-done | bytes 1990672 | tf_op jit(solution)/shard_map/reduce_scatter | solution.py:304
  762.7 103.8 %reduce-scatter.27.cloned.1.call-done = bf16[288,4608]{1,0:T(8,128)(2,1)} async-done(((bf16[1152,4608]{1,0:T(8,128)(2,1)}), bf16[288,4608]{1,0:T(8,128)(2,1)}) %reduce-scatter.27.cloned.1.call-update) | async-done | bytes 2654224 | tf_op jit(solution)/shard_map/reduce_scatter | solution.py:310
  871.3 103.1 %reduce-scatter.29.cloned.1.call-done = bf16[1152,1152]{1,0:T(8,128)(2,1)} async-done(((bf16[4608,1152]{1,0:T(8,128)(2,1)}), bf16[1152,1152]{1,0:T(8,128)(2,1)}) %reduce-scatter.29.cloned.1.call-update) | async-done | bytes 2654224 | tf_op jit(solution)/shard_map/reduce_scatter | solution.py:313
  979.7 145.4 %reduce-scatter.21.cloned.1.call-done = bf16[288,6912]{1,0:T(8,128)(2,1)} async-done(((bf16[1152,6912]{1,0:T(8,128)(2,1)}), bf16[288,6912]{1,0:T(8,128)(2,1)}) %reduce-scatter.21.cloned.1.call-update) | async-done | bytes 3981328 | tf_op jit(solution)/shard_map/reduce_scatter | solution.py:301
  1146.1 29.3 %all-reduce.13 = (bf16[6912]{0:T(1024)(128)(2,1)S(1)}, bf16[1152]{0:T(1024)(128)(2,1)S(1)}, bf16[1152]{0:T(1024)(128)(2,1)S(1)}, bf16[1152]{0:T(1024)(128)(2,1)S...) all-reduce(bf16[6912]{0:T(1024)(128)(2,1)S(1)} %copy-done.57, ...), channel_id=4, replica_groups=mesh['dp'=4,'fsdp'=8] {'fsdp'}, use_global_device_ids=true, to_apply=%region_28.29.clone | all-reduce | flops 16128 | bytes 64512
  1175.9 9.1 all-reduce.15
  1191.1 7.8 fusion.89
  1203.3 40.1 %reduce-scatter.37.cloned.1.call-done = bf16[576,288]{1,0:T(8,128)(2,1)} async-done(((bf16[4608,288]{1,0:T(8,128)(2,1)}), bf16[576,288]{1,0:T(8,128)(2,1)}) %reduce-scatter.37.cloned.1.call-update) | async-done | bytes 331792
  1245.6 36.3 %reduce-scatter.39.cloned.1.call-done = bf16[144,1152]{1,0:T(8,128)(2,1)} async-done(((bf16[1152,1152]{1,0:T(8,128)(2,1)}), bf16[144,1152]{1,0:T(8,128)(2,1)}) %reduce-scatter.39.cloned.1.call-update) | async-done | bytes 331792
  1284.3 59.5 %reduce-scatter.31.cloned.1.call-done = bf16[864,288]{1,0:T(8,128)(2,1)} async-done(((bf16[6912,288]{1,0:T(8,128)(2,1)}), bf16[864,288]{1,0:T(8,128)(2,1)}) %reduce-scatter.31.cloned.1.call-update) | async-done | bytes 497680
  (427 shorter events, 154.8 us)
Async XLA Ops:
  7.2 146.8 %copy-start = (bf16[1,256,1152]{2,1,0:T(8,128)(2,1)S(1)}, bf16[1,256,1152]{2,1,0:T(8,128)(2,1)}, u32[]{:S(2)}) copy-start(bf16[1,256,1152]{2,1,0:T(8,128)(2,1)} %param.19) | copy-start | bytes 1769476
  7.2 40.5 %all-gather.10.cloned.1.call-start = ((), (), s32[]{:S(2)}) async-start(), calls=%async_computation.10 | async-start | bytes 2580480 | tf_op jit(solution)/shard_map/all_gather | solution.py:138
  7.9 79.0 %all-gather.18.cloned.1.call-start = ((), (), s32[]{:S(2)}) async-start(), calls=%async_computation.14 | async-start | bytes 1843200 | tf_op jit(solution)/shard_map/all_gather | solution.py:141
  8.7 108.8 %all-gather.22.cloned.1.call-start = ((), (), s32[]{:S(2)}) async-start(), calls=%async_computation.16 | async-start | bytes 1658880 | tf_op jit(solution)/shard_map/all_gather | solution.py:142
  9.4 254.5 %all-gather.12.cloned.1.call-start = ((), (), s32[]{:S(2)}) async-start(), calls=%async_computation.11 | async-start | bytes 17915904 | tf_op jit(solution)/shard_map/all_gather | solution.py:145
  51.8 291.0 %all-gather.14.cloned.1.call-start = ((), (), s32[]{:S(2)}) async-start(), calls=%async_computation.12 | async-start | bytes 8957952 | tf_op jit(solution)/shard_map/all_gather | solution.py:146
  71.6 306.0 %all-gather.16.cloned.1.call-start = ((), (), s32[]{:S(2)}) async-start(), calls=%async_computation.13 | async-start | bytes 2985984 | tf_op jit(solution)/shard_map/all_gather | solution.py:147
  86.8 392.0 %all-gather.20.cloned.1.call-start = ((), (), s32[]{:S(2)}) async-start(), calls=%async_computation.15 | async-start | bytes 11943936 | tf_op jit(solution)/shard_map/all_gather | solution.py:148
  89.6 64.4 %copy-start.113 = (s32[1,128]{1,0:T(1,128)S(1)}, s32[1,128]{1,0:T(1,128)}, u32[]{:S(2)}) copy-start(s32[1,128]{1,0:T(1,128)} %param.20) | copy-start | bytes 1540
  89.6 489.7 %all-gather.24.cloned.1.call-start = ((), (), s32[]{:S(2)}) async-start(), calls=%async_computation.17 | async-start | bytes 11943936 | tf_op jit(solution)/shard_map/all_gather | solution.py:149
  117.5 610.2 %reduce-scatter.25.cloned.1.call-start = ((), (), s32[]{:S(2)}) async-start(), calls=%async_computation.20 | async-start | bytes 3317760 | tf_op jit(solution)/shard_map/reduce_scatter | solution.py:307
  154.9 108.9 %copy-start.58 = (bf16[1,1152]{1,0:T(2,128)(2,1)S(1)}, bf16[1,1152]{1,0:T(2,128)(2,1)}, u32[]{:S(2)}) copy-start(bf16[1,1152]{1,0:T(2,128)(2,1)} %param.22) | copy-start | bytes 6916
  155.0 108.9 %copy-start.61 = (bf16[1,1152]{1,0:T(2,128)(2,1)S(1)}, bf16[1,1152]{1,0:T(2,128)(2,1)}, u32[]{:S(2)}) copy-start(bf16[1,1152]{1,0:T(2,128)(2,1)} %param.21) | copy-start | bytes 6916
  155.3 187.8 %copy-start.94 = (f32[384]{0:T(512)}, f32[384]{0:T(512)S(1)}, u32[]{:S(2)}) copy-start(f32[384]{0:T(512)S(1)} %broadcast_multiply_fusion.5) | copy-start | bytes 4612
  155.7 187.4 %copy-start.102 = (f32[384]{0:T(512)}, f32[384]{0:T(512)S(1)}, u32[]{:S(2)}) copy-start(f32[384]{0:T(512)S(1)} %add_rsqrt_fusion.1) | copy-start | bytes 4612
  156.0 187.1 %copy-start.20 = (bf16[128,1152]{1,0:T(8,128)(2,1)}, bf16[128,1152]{1,0:T(8,128)(2,1)S(1)}, u32[]{:S(2)}) copy-start(bf16[128,1152]{1,0:T(8,128)(2,1)S(1)} %broadcast_select_fusion) | copy-start | bytes 884740
  274.4 68.8 %copy-start.49 = (f32[1152]{0:T(1024)}, f32[1152]{0:T(1024)S(1)}, u32[]{:S(2)}) copy-start(f32[1152]{0:T(1024)S(1)} %get-tuple-element.117) | copy-start | bytes 13828
  274.4 68.8 %copy-start.51 = (f32[1152]{0:T(1024)}, f32[1152]{0:T(1024)S(1)}, u32[]{:S(2)}) copy-start(f32[1152]{0:T(1024)S(1)} %get-tuple-element.116) | copy-start | bytes 13828
  274.4 68.8 %copy-start.53 = (f32[1152]{0:T(1024)}, f32[1152]{0:T(1024)S(1)}, u32[]{:S(2)}) copy-start(f32[1152]{0:T(1024)S(1)} %get-tuple-element.115) | copy-start | bytes 13828
  274.4 68.8 %copy-start.55 = (f32[1152]{0:T(1024)}, f32[1152]{0:T(1024)S(1)}, u32[]{:S(2)}) copy-start(f32[1152]{0:T(1024)S(1)} %get-tuple-element.114) | copy-start | bytes 13828
  274.4 304.9 %copy-start.47 = (f32[1152]{0:T(1024)}, f32[1152]{0:T(1024)S(1)}, u32[]{:S(2)}) copy-start(f32[1152]{0:T(1024)S(1)} %get-tuple-element.113) | copy-start | bytes 13828
  274.4 305.0 %copy-start.45 = (f32[1152]{0:T(1024)}, f32[1152]{0:T(1024)S(1)}, u32[]{:S(2)}) copy-start(f32[1152]{0:T(1024)S(1)} %get-tuple-element.108) | copy-start | bytes 13828
  632.6 125.8 %reduce-scatter.23.cloned.1.call-start = ((), (), s32[]{:S(2)}) async-start(), calls=%async_computation.19 | async-start | bytes 9953280 | tf_op jit(solution)/shard_map/reduce_scatter | solution.py:304
  676.3 190.2 %reduce-scatter.27.cloned.1.call-start = ((), (), s32[]{:S(2)}) async-start(), calls=%async_computation.21 | async-start | bytes 13271040 | tf_op jit(solution)/shard_map/reduce_scatter | solution.py:310
  688.7 285.7 %reduce-scatter.29.cloned.1.call-start = ((), (), s32[]{:S(2)}) async-start(), calls=%async_computation.22 | async-start | bytes 13271040 | tf_op jit(solution)/shard_map/reduce_scatter | solution.py:313
  701.8 423.3 %reduce-scatter.21.cloned.1.call-start = ((), (), s32[]{:S(2)}) async-start(), calls=%async_computation.18 | async-start | bytes 19906560 | tf_op jit(solution)/shard_map/reduce_scatter | solution.py:301
  727.7 471.8 %reduce-scatter.35.cloned.1.call-start = ((), (), s32[]{:S(2)}) async-start(), calls=%async_computation.25 | async-start | bytes 995328
  730.1 471.2 %reduce-scatter.33.cloned.1.call-start = ((), (), s32[]{:S(2)}) async-start(), calls=%async_computation.24 | async-start | bytes 2985984
  762.6 480.8 %reduce-scatter.37.cloned.1.call-start = ((), (), s32[]{:S(2)}) async-start(), calls=%async_computation.26 | async-start | bytes 3981312
  871.2 410.7 %reduce-scatter.39.cloned.1.call-start = ((), (), s32[]{:S(2)}) async-start(), calls=%async_computation.27 | async-start | bytes 2985984
  979.6 364.1 %reduce-scatter.31.cloned.1.call-start = ((), (), s32[]{:S(2)}) async-start(), calls=%async_computation.23 | async-start | bytes 5971968
  1281.9 64.2 %copy-start.1 = (bf16[1,256,1152]{2,1,0:T(8,128)(2,1)S(1)}, bf16[1,256,1152]{2,1,0:T(8,128)(2,1)}, u32[]{:S(2)}) copy-start(bf16[1,256,1152]{2,1,0:T(8,128)(2,1)} %param.19) | copy-start | bytes 1769476
  (105 other events, 753.5 us)
Sparse Core Ops, SparseCore 0:
  9.9 37.7 all-gather.9
  49.5 37.1 all-gather.17
  88.5 28.9 all-gather.21
  119.0 144.8 all-gather.11
  265.9 76.8 all-gather.13
  344.9 32.7 all-gather.15
  379.3 99.4 all-gather.19
  480.4 98.8 all-gather.23
  632.8 38.2 reduce-scatter.24
  676.4 81.9 reduce-scatter.22
  761.8 104.6 reduce-scatter.26
  869.7 104.6 reduce-scatter.28
  977.8 147.2 reduce-scatter.20
  1127.8 32.1 reduce-scatter.34
  1162.2 35.9 reduce-scatter.32
  1200.5 42.8 reduce-scatter.36
  1245.6 36.2 reduce-scatter.38
  1284.1 59.6 reduce-scatter.30
where the time goes:
time: 1360 us; the launch traced here: 1350 us
  waiting for transfers between devices  943 us (69%)
  matrix products  169 us (12%)
  blocking collectives  100 us (7%)
  local copies, waits for them, and re-layouts  83.4 us (6%)
  other arithmetic  36.9 us (3%)
  between operations  19.9 us (1%)
    reduce_scatter x1, waiting for transfers between devices, on_device(): lax.psum_scatter(grad_w_ada.astype(jnp.bfloat16), 'dp', scatter_dimension...  145 us
    unnamed x23, waiting for transfers between devices  138 us
    all_gather x1, waiting for transfers between devices, on_device(): lax.all_gather(row_blocks[0], 'fsdp', axis=1, tiled=True)  107 us
    reduce_scatter x1, waiting for transfers between devices, on_device(): lax.psum_scatter(grad_w_fc1.astype(jnp.bfloat16), 'dp', scatter_dimension...  104 us
    reduce_scatter x1, waiting for transfers between devices, on_device(): lax.psum_scatter(grad_w_fc2.astype(jnp.bfloat16), 'dp', scatter_dimension...  103 us
    all_gather x1, waiting for transfers between devices, on_device(): lax.all_gather(row_blocks[3], 'fsdp', axis=1, tiled=True)  93.7 us
    all_gather x1, waiting for transfers between devices, on_device(): lax.all_gather(row_blocks[4], 'fsdp', axis=1, tiled=True)  81.7 us
    all_gather x1, waiting for transfers between devices, on_device(): lax.all_gather(row_blocks[1], 'fsdp', axis=1, tiled=True)  68.4 us
  transfers between devices with their start and end apart: 18, of which 14 were waited for; matrix products, arithmetic and copies ran while one was open for 16% of the time, Pallas kernels for 0%

commit v1 on v0

--- a/solution.py
+++ b/solution.py
@@ -1,9 +1,14 @@
 import math
+import functools
 
 import jax
 import jax.numpy as jnp
 from jax import lax
+from jax.experimental import pallas as pl
+from jax.experimental.pallas import tpu as pltpu
 from jax.sharding import PartitionSpec as P
+
+MESH = pl.DeviceIdType.MESH
 
 HEAD_DIM = 72
 
@@ -114,7 +119,252 @@
     )
 
 
+MATS = (("qkv", 864, True), ("out", 288, False), ("fc1", 1152, True), ("fc2", 1152, False))
+SPLIT = ((80, 64), (64, 80))
+
+
+class Place:
+    def __init__(self):
+        self.dp = lax.axis_index("dp")
+        self.f = lax.axis_index("fsdp")
+        self.z = self.f // 2
+        self.c = self.f % 2
+        dp, f = self.dp, self.f
+        self.xn = dp + 1 - 2 * (dp % 2)
+        self.yn = (dp + 2) % 4
+        self.dg = 3 - dp
+        self.sib_f = f + 1 - 2 * self.c
+        self.middle = (self.z == 1) | (self.z == 2)
+        z = self.z
+        low = z < 2
+        self.order = (
+            z,
+            z + 1 - 2 * (z % 2),
+            jnp.where(low, 2, 1),
+            jnp.where(low, 3, 0),
+        )
+
+
+def barrier_all(p):
+    sem = pltpu.get_barrier_semaphore()
+    for dev in ((p.xn, p.f), (p.yn, p.f), (p.dp, p.sib_f)):
+        pl.semaphore_signal(sem, inc=1, device_id=dev, device_id_type=MESH)
+
+    @pl.when(p.z < 3)
+    def _():
+        pl.semaphore_signal(sem, inc=1, device_id=(p.dp, p.f + 2), device_id_type=MESH)
+
+    @pl.when(p.z > 0)
+    def _():
+        pl.semaphore_signal(sem, inc=1, device_id=(p.dp, p.f - 2), device_id_type=MESH)
+
+    pl.semaphore_wait(sem, jnp.where(p.middle, 5, 4))
+
+
+class Gather:
+    def __init__(self, p, bufs, sems):
+        self.p, self.bufs = p, bufs
+        (self.rz, self.rx, self.ry, self.rd, self.rs, self.so, self.sf, self.sx, self.sy, self.sd, self.ss, self.loc) = sems
+
+    def slot(self, m, dp, zs):
+        t = self.bufs[m]
+        return t.at[zs, dp, self.p.c] if MATS[m][2] else t.at[dp, zs, self.p.c]
+
+    def plane(self, m, zs):
+        t = self.bufs[m]
+        return t.at[zs, :, self.p.c] if MATS[m][2] else t.at[:, zs, self.p.c]
+
+    def cp(self, src, dst, send, recv, dev):
+        return pltpu.make_async_remote_copy(src_ref=src, dst_ref=dst, send_sem=send, recv_sem=recv, device_id=dev, device_id_type=MESH)
+
+    def z_copy(self, m, src, zs, send, step):
+        p = self.p
+        return self.cp(src, self.slot(m, p.dp, zs), send, self.rz.at[m, zs], (p.dp, p.f + step))
+
+    def x_copy(self, m, src, zs):
+        p = self.p
+        return self.cp(src, self.slot(m, p.dp, zs), self.sx.at[m, zs], self.rx.at[m, zs], (p.xn, p.f))
+
+    def y_copy(self, m, src, zs):
+        p = self.p
+        return self.cp(src, self.slot(m, p.dp, zs), self.sy.at[m, zs], self.ry.at[m, zs], (p.yn, p.f))
+
+    def d_copy(self, m, j, zs, half):
+        p = self.p
+        a, b = SPLIT[j % 2]
+        rows = pl.ds(0, a) if half == 0 else pl.ds(a, b)
+        src = self.slot(m, p.xn if half == 0 else p.yn, zs).at[rows]
+        dev = (p.yn, p.f) if half == 0 else (p.xn, p.f)
+        return self.cp(src, src, self.sd.at[m, zs, half], self.rd.at[m, zs, half], dev)
+
+    def d_wait(self, m, j, zs, half):
+        p = self.p
+        a, b = SPLIT[j % 2]
+        rows = pl.ds(0, a) if half == 0 else pl.ds(a, b)
+        dst = self.slot(m, p.dg, zs).at[rows]
+        self.cp(dst, dst, self.sd.at[m, zs, half], self.rd.at[m, zs, half], (p.xn, p.f)).wait_recv()
+
+    def s_copy(self, m, zs):
+        p = self.p
+        src = self.plane(m, zs)
+        return self.cp(src, src, self.ss.at[m, zs], self.rs.at[m, zs], (p.dp, p.sib_f))
+
+    def own(self, m, blk):
+        p = self.p
+
+        @pl.when(p.z < 3)
+        def _():
+            self.z_copy(m, blk, p.z, self.so.at[m, 0], 2).start()
+
+        @pl.when(p.z > 0)
+        def _():
+            self.z_copy(m, blk, p.z, self.so.at[m, 1], -2).start()
+
+        self.x_copy(m, blk, p.z).start()
+        self.y_copy(m, blk, p.z).start()
+        pltpu.make_async_copy(blk, self.slot(m, p.dp, p.z), self.loc.at[m]).start()
+
+    def arrive(self, m, j):
+        p = self.p
+        zs = p.order[j]
+        slot = self.slot(m, p.dp, zs)
+        self.cp(slot, slot, self.sf.at[m, zs], self.rz.at[m, zs], (p.xn, p.f)).wait_recv()
+
+        @pl.when(p.middle)
+        def _():
+            step = jnp.where(zs < p.z, 2, -2)
+            self.z_copy(m, slot, zs, self.sf.at[m, zs], step).start()
+
+        self.x_copy(m, slot, zs).start()
+        self.y_copy(m, slot, zs).start()
+
+    def cross(self, m, j):
+        p = self.p
+        zs = p.order[j]
+        sx, sy = self.slot(m, p.xn, zs), self.slot(m, p.yn, zs)
+        self.cp(sx, sx, self.sx.at[m, zs], self.rx.at[m, zs], (p.xn, p.f)).wait_recv()
+        self.d_copy(m, j, zs, 0).start()
+        self.cp(sy, sy, self.sy.at[m, zs], self.ry.at[m, zs], (p.yn, p.f)).wait_recv()
+        self.d_copy(m, j, zs, 1).start()
+
+    def finish(self, m, j):
+        p = self.p
+        zs = p.order[j]
+        self.d_wait(m, j, zs, 0)
+        self.d_wait(m, j, zs, 1)
+        if j == 0:
+            pltpu.make_async_copy(self.slot(m, p.dp, p.z), self.slot(m, p.dp, p.z), self.loc.at[m]).wait()
+        self.s_copy(m, zs).start()
+
+    def arrived(self, m, j):
+        p = self.p
+        dst = self.plane(m, p.order[j])
+        other = self.bufs[m].at[p.order[j], :, 1 - p.c] if MATS[m][2] else self.bufs[m].at[:, p.order[j], 1 - p.c]
+        self.cp(dst, other, self.ss.at[m, p.order[j]], self.rs.at[m, p.order[j]], (p.dp, p.sib_f)).wait_recv()
+
+    def drain(self, m, blk):
+        p = self.p
+
+        @pl.when(p.z < 3)
+        def _():
+            self.z_copy(m, blk, p.z, self.so.at[m, 0], 2).wait_send()
+
+        @pl.when(p.z > 0)
+        def _():
+            self.z_copy(m, blk, p.z, self.so.at[m, 1], -2).wait_send()
+
+        for j in range(4):
+            zs = p.order[j]
+            src = self.slot(m, p.dp, zs)
+            if j:
+                @pl.when(p.middle)
+                def _():
+                    step = jnp.where(zs < p.z, 2, -2)
+                    self.z_copy(m, src, zs, self.sf.at[m, zs], step).wait_send()
+            self.x_copy(m, src, zs).wait_send()
+            self.y_copy(m, src, zs).wait_send()
+            self.d_copy(m, j, zs, 0).wait_send()
+            self.d_copy(m, j, zs, 1).wait_send()
+            self.s_copy(m, zs).wait_send()
+
+
+def gather_sems():
+    D = pltpu.SemaphoreType.DMA
+    return [D((4, 4)), D((4, 4)), D((4, 4)), D((4, 4, 2)), D((4, 4)), D((4, 2)), D((4, 4)), D((4, 4)), D((4, 4)), D((4, 4, 2)), D((4, 4)), D((4,))]
+
+
+N_SEMS = 12
+
+
+def stage(p, shard, got, width, send, recv):
+    rows = shard.shape[0] // 2
+    return pltpu.make_async_remote_copy(
+        src_ref=shard.at[pl.ds((1 - p.c) * rows, rows)], dst_ref=got, send_sem=send, recv_sem=recv,
+        device_id=(p.dp, p.sib_f), device_id_type=MESH)
+
+
+def join(p, shard, got, blk):
+    rows, width = got.shape
+    own = shard[pl.ds(pl.multiple_of(p.c * rows, 16), rows), :]
+    other = got[...]
+    first = p.c == 0
+    blk[:, 0:width] = jnp.where(first, own, other)
+    blk[:, width:2 * width] = jnp.where(first, other, own)
+
+
+def ag_kernel(wq, wo, w1, w2, tq, to, t1, t2, gq, g1, bq, b1, ssem, rsem, *sems):
+    p = Place()
+    g = Gather(p, (tq, to, t1, t2), sems)
+    blks = (bq, wo, b1, w2)
+    barrier_all(p)
+    cq = stage(p, wq, gq, 432, ssem.at[0], rsem.at[0])
+    cq.start()
+    c1 = stage(p, w1, g1, 576, ssem.at[1], rsem.at[1])
+    c1.start()
+    g.own(1, wo)
+    cq.wait_recv()
+    join(p, wq, gq, bq)
+    g.own(0, bq)
+    c1.wait_recv()
+    join(p, w1, g1, b1)
+    for m in range(4):
+        if m + 1 < 4 and m + 1 >= 2:
+            g.own(m + 1, blks[m + 1])
+        for j in range(5):
+            if 1 <= j <= 3:
+                g.arrive(m, j)
+            if j >= 1:
+                g.cross(m, j - 1)
+            if j >= 2:
+                g.finish(m, j - 2)
+        g.finish(m, 3)
+        for j in range(4):
+            g.arrived(m, j)
+    cq.wait_send()
+    c1.wait_send()
+    for m in range(4):
+        g.drain(m, blks[m])
+
+
+def all_gather(w_qkv, w_out, w_fc1, w_fc2):
+    B = jnp.bfloat16
+    shapes = [jax.ShapeDtypeStruct((4, 4, 2, 144, n), B) for _, n, _ in MATS]
+    V = pl.BlockSpec(memory_space=pltpu.VMEM)
+    outs = pl.pallas_call(
+        ag_kernel,
+        out_shape=shapes,
+        in_specs=[V] * 4,
+        out_specs=[pl.BlockSpec(memory_space=pl.ANY)] * 4,
+        scratch_shapes=[pltpu.VMEM((144, 432), B), pltpu.VMEM((144, 576), B), pltpu.VMEM((144, 864), B), pltpu.VMEM((144, 1152), B),
+                        pltpu.SemaphoreType.DMA((2,)), pltpu.SemaphoreType.DMA((2,))] + gather_sems(),
+        compiler_params=pltpu.CompilerParams(collective_id=0, has_side_effects=True, vmem_limit_bytes=32 * 2**20),
+        name="gather_weights",
+    )(w_qkv, w_out.T, w_fc1, w_fc2.T)
+    return outs
+
+
 def on_device(
+    special,
     full_input,
     masked_input,
     keep_index,
@@ -134,28 +384,22 @@
     cot_full,
     cot_masked,
 ):
-    row_blocks = (
-        lax.all_gather(w_ada, "dp", axis=0, tiled=True),
-        lax.all_gather(w_qkv, "dp", axis=0, tiled=True),
-        lax.all_gather(w_out, "dp", axis=0, tiled=True),
-        lax.all_gather(w_fc1, "dp", axis=0, tiled=True),
-        lax.all_gather(w_fc2, "dp", axis=0, tiled=True),
-    )
-    gathered = (
-        lax.all_gather(row_blocks[0], "fsdp", axis=1, tiled=True),
-        lax.all_gather(row_blocks[1], "fsdp", axis=1, tiled=True),
-        lax.all_gather(row_blocks[2], "fsdp", axis=1, tiled=True),
-        lax.all_gather(row_blocks[3], "fsdp", axis=1, tiled=True),
-        lax.all_gather(row_blocks[4], "fsdp", axis=1, tiled=True),
-        lax.all_gather(b_ada, "fsdp", axis=0, tiled=True),
-        lax.all_gather(b_q, "fsdp", axis=0, tiled=True),
-        lax.all_gather(b_v, "fsdp", axis=0, tiled=True),
-        lax.all_gather(b_out, "fsdp", axis=0, tiled=True),
-        lax.all_gather(b_fc1, "fsdp", axis=0, tiled=True),
-        lax.all_gather(b_fc2, "fsdp", axis=0, tiled=True),
-    )
-    weights = gathered[:5]
-    biases = gathered[5:]
+    def columns(shard):
+        return lax.all_gather(lax.all_gather(shard, "dp", axis=0, tiled=True), "fsdp", axis=1, tiled=True)
+
+    if special:
+        bufs = all_gather(w_qkv, w_out, w_fc1, w_fc2)
+        flat = [t.reshape(4, 1152, -1) for t in bufs]
+        qkv, out_t, fc1, fc2_t = [jnp.concatenate(list(t), axis=1) for t in flat]
+        weights = (None, qkv, out_t.T, fc1, fc2_t.T)
+    else:
+        weights = (None, columns(w_qkv), columns(w_out), columns(w_fc1), columns(w_fc2))
+    widths = [b.shape[0] for b in (b_q, b_v, b_out, b_fc1, b_fc2)]
+    packed = lax.all_gather(jnp.concatenate([b_q, b_v, b_out, b_fc1, b_fc2]), "fsdp", axis=0, tiled=False)
+    biases, at = [None], 0
+    for width in widths:
+        biases.append(packed[:, at : at + width].reshape(-1))
+        at += width
     full_length = full_input.shape[1]
     images = full_input.shape[0]
     features = full_input.shape[2]
@@ -163,34 +407,16 @@
     tokens = jnp.concatenate([full_input, picked], axis=1).astype(jnp.float32)
     conds = jnp.stack([cond_full, cond_masked], axis=1).astype(jnp.float32)
     silu_low = jax.nn.silu(conds).astype(jnp.bfloat16)
-    mods = jnp.einsum(
-        "ijd,de->ije", silu_low, weights[0], preferred_element_type=jnp.float32
-    ) + biases[0].astype(jnp.float32)
-    result = forward_pass(tokens, mods, weights, biases, full_length)[0]
-    again_rows = (
-        lax.all_gather(w_ada, "dp", axis=0, tiled=True),
-        lax.all_gather(w_qkv, "dp", axis=0, tiled=True),
-        lax.all_gather(w_out, "dp", axis=0, tiled=True),
-        lax.all_gather(w_fc1, "dp", axis=0, tiled=True),
-        lax.all_gather(w_fc2, "dp", axis=0, tiled=True),
-    )
-    again = (
-        lax.all_gather(again_rows[0], "fsdp", axis=1, tiled=True),
-        lax.all_gather(again_rows[1], "fsdp", axis=1, tiled=True),
-        lax.all_gather(again_rows[2], "fsdp", axis=1, tiled=True),
-        lax.all_gather(again_rows[3], "fsdp", axis=1, tiled=True),
-        lax.all_gather(again_rows[4], "fsdp", axis=1, tiled=True),
-        lax.all_gather(b_ada, "fsdp", axis=0, tiled=True),
-        lax.all_gather(b_q, "fsdp", axis=0, tiled=True),
-        lax.all_gather(b_v, "fsdp", axis=0, tiled=True),
-        lax.all_gather(b_out, "fsdp", axis=0, tiled=True),
-        lax.all_gather(b_fc1, "fsdp", axis=0, tiled=True),
-        lax.all_gather(b_fc2, "fsdp", axis=0, tiled=True),
-    )
-    weights = again[:5]
-    biases = again[5:]
+    n_dp, n_fsdp = lax.axis_size("dp"), lax.axis_size("fsdp")
+    rows_ada, cols_ada = w_ada.shape
+    every_silu = lax.all_gather(silu_low, ("dp", "fsdp"), axis=0, tiled=True)
+    my_silu = lax.dynamic_slice_in_dim(every_silu, lax.axis_index("dp") * rows_ada, rows_ada, axis=2)
+    part = jnp.einsum("ijd,de->ije", my_silu, w_ada, preferred_element_type=jnp.float32)
+    part = lax.psum_scatter(part, "dp", scatter_dimension=0, tiled=True)
+    part = part + b_ada.astype(jnp.float32)
+    mods = lax.all_to_all(part, "fsdp", split_axis=0, concat_axis=2, tiled=True)
     (
-        recomputed,
+        result,
         pieces,
         norm_one,
         inverse_one,
@@ -287,9 +513,14 @@
         ],
         axis=-1,
     ).astype(jnp.bfloat16)
-    grad_b_ada = jnp.sum(grad_mods.astype(jnp.float32), axis=(0, 1))
-    grad_w_ada = jnp.einsum("ijd,ije->de", silu_low, grad_mods, preferred_element_type=jnp.float32)
-    grad_silu = jnp.einsum("ije,de->ijd", grad_mods, weights[0], preferred_element_type=jnp.float32)
+    cut = grad_mods.reshape(images, 2, n_fsdp, cols_ada)
+    mine = lax.all_to_all(cut, "fsdp", split_axis=2, concat_axis=0, tiled=False)
+    mine = lax.all_gather(mine.reshape(n_fsdp * images, 2, cols_ada), "dp", axis=0, tiled=True)
+    grad_b_ada = jnp.sum(mine.astype(jnp.float32), axis=(0, 1))
+    grad_w_ada = jnp.einsum("ijd,ije->de", my_silu, mine, preferred_element_type=jnp.float32)
+    back = jnp.einsum("ije,de->ijd", mine, w_ada, preferred_element_type=jnp.float32)
+    back = lax.psum_scatter(back.reshape(n_dp, n_fsdp * images, 2, rows_ada), "fsdp", scatter_dimension=1, tiled=True)
+    grad_silu = lax.all_to_all(back, "dp", split_axis=0, concat_axis=3, tiled=True).reshape(images, 2, features)
     grad_cond = jax.vjp(jax.nn.silu, conds)[1](grad_silu)[0]
     image_rows = jnp.arange(images)[:, None]
     grad_masked = (
@@ -297,68 +528,18 @@
         .at[image_rows, keep_index]
         .set(grad_tokens[:, full_length:])
     )
-    inner = (
-        lax.psum_scatter(
-            grad_w_ada.astype(jnp.bfloat16), "dp", scatter_dimension=0, tiled=True
-        ).astype(jnp.float32),
-        lax.psum_scatter(
-            grad_w_qkv.astype(jnp.bfloat16), "dp", scatter_dimension=0, tiled=True
-        ).astype(jnp.float32),
-        lax.psum_scatter(
-            grad_w_out.astype(jnp.bfloat16), "dp", scatter_dimension=0, tiled=True
-        ).astype(jnp.float32),
-        lax.psum_scatter(
-            grad_w_fc1.astype(jnp.bfloat16), "dp", scatter_dimension=0, tiled=True
-        ).astype(jnp.float32),
-        lax.psum_scatter(
-            grad_w_fc2.astype(jnp.bfloat16), "dp", scatter_dimension=0, tiled=True
-        ).astype(jnp.float32),
-    )
-    totals = (
-        lax.psum(grad_b_ada.astype(jnp.bfloat16), "dp").astype(jnp.float32),
-        lax.psum(grad_b_q.astype(jnp.bfloat16), "dp").astype(jnp.float32),
-        lax.psum(grad_b_v.astype(jnp.bfloat16), "dp").astype(jnp.float32),
-        lax.psum(grad_b_out.astype(jnp.bfloat16), "dp").astype(jnp.float32),
-        lax.psum(grad_b_fc1.astype(jnp.bfloat16), "dp").astype(jnp.float32),
-        lax.psum(grad_b_fc2.astype(jnp.bfloat16), "dp").astype(jnp.float32),
-    )
-    summed = (
-        lax.psum_scatter(
-            inner[0].astype(jnp.bfloat16), "fsdp", scatter_dimension=1, tiled=True
-        ).astype(jnp.float32),
-        lax.psum_scatter(
-            inner[1].astype(jnp.bfloat16), "fsdp", scatter_dimension=1, tiled=True
-        ).astype(jnp.float32),
-        lax.psum_scatter(
-            inner[2].astype(jnp.bfloat16), "fsdp", scatter_dimension=1, tiled=True
-        ).astype(jnp.float32),
-        lax.psum_scatter(
-            inner[3].astype(jnp.bfloat16), "fsdp", scatter_dimension=1, tiled=True
-        ).astype(jnp.float32),
-        lax.psum_scatter(
-            inner[4].astype(jnp.bfloat16), "fsdp", scatter_dimension=1, tiled=True
-        ).astype(jnp.float32),
-        lax.psum_scatter(
-            totals[0].astype(jnp.bfloat16), "fsdp", scatter_dimension=0, tiled=True
-        ).astype(jnp.float32),
-        lax.psum_scatter(
-            totals[1].astype(jnp.bfloat16), "fsdp", scatter_dimension=0, tiled=True
-        ).astype(jnp.float32),
-        lax.psum_scatter(
-            totals[2].astype(jnp.bfloat16), "fsdp", scatter_dimension=0, tiled=True
-        ).astype(jnp.float32),
-        lax.psum_scatter(
-            totals[3].astype(jnp.bfloat16), "fsdp", scatter_dimension=0, tiled=True
-        ).astype(jnp.float32),
-        lax.psum_scatter(
-            totals[4].astype(jnp.bfloat16), "fsdp", scatter_dimension=0, tiled=True
-        ).astype(jnp.float32),
-        lax.psum_scatter(
-            totals[5].astype(jnp.bfloat16), "fsdp", scatter_dimension=0, tiled=True
-        ).astype(jnp.float32),
-    )
-    matrices = summed[:5]
-    vectors = summed[5:]
+    def owned(grad):
+        inner = lax.psum_scatter(grad.astype(jnp.bfloat16), "dp", scatter_dimension=0, tiled=True)
+        return lax.psum_scatter(inner, "fsdp", scatter_dimension=1, tiled=True).astype(jnp.float32)
+
+    matrices = (grad_w_ada, owned(grad_w_qkv), owned(grad_w_out), owned(grad_w_fc1), owned(grad_w_fc2))
+    sums = (grad_b_q, grad_b_v, grad_b_out, grad_b_fc1, grad_b_fc2)
+    line = jnp.concatenate([g.reshape(n_fsdp, -1) for g in sums], axis=1)
+    line = lax.psum(lax.psum_scatter(line, "fsdp", scatter_dimension=0, tiled=True), "dp")[0]
+    vectors, at = [grad_b_ada], 0
+    for width in widths:
+        vectors.append(line[at : at + width])
+        at += width
     return (
         result[:, :full_length].astype(jnp.bfloat16),
         result[:, full_length:].astype(jnp.bfloat16),
@@ -381,8 +562,9 @@
 
 
 def solution(mesh):
+    special = dict(mesh.shape) == {"dp": 4, "fsdp": 8}
     return jax.shard_map(
-        on_device,
+        functools.partial(on_device, special),
         mesh=mesh,
         in_specs=(
             P(("dp", "fsdp"), None, None),

time: 1360 us -> 974 us (0.72)
  waiting for transfers between devices: 943 us -> 377 us
  Pallas kernels: 0 us -> 156 us
  local copies, waits for them, and re-layouts: 83.4 us -> 112 us
    all_gather x8 -> x0, waiting for transfers between devices: 424 us -> none  [the longest x1 107 us: on_device(): lax.all_gather(row_blocks[0], 'fsdp', axis=1, tiled=True)]
    pallas_call x0 -> x1, Pallas kernels: none -> 156 us  [all_gather(): pl.pallas_call(ag_kernel, out_shape=shapes, in_specs=[V] * 4, out_specs=[...]
    reduce_scatter x5, waiting for transfers between devices: 381 us -> 226 us  [the longest x4 226 us: owned(): lax.psum_scatter(grad.astype(jnp.bfloat16), 'dp', scatter_dimension=0, ti...]
    all_gather x2 -> x3, blocking collectives: 31.3 us -> 64.9 us  [the longest x1 43.8 us: on_device(): every_silu = lax.all_gather(silu_low, ('dp', 'fsdp'), axis=0, tiled=True)]
    unnamed x2 -> x1, blocking collectives: 59.9 us -> 28.9 us
    dot_general x3, matrix products: 25.4 us -> 3.53 us  [the longest x1 1.95 us: on_device(): jnp.einsum('ijd,de->ije', my_silu, w_ada, preferred_element_type=jnp.floa...]
    concatenate x0 -> x6, local copies, waits for them, and re-layouts: none -> 20.7 us  [the longest x2 19.6 us: on_device(): qkv, out_t, fc1, fc2_t = [jnp.concatenate(list(t), axis=1) for t in flat]]
    another operation x0 -> x3, local copies, waits for them, and re-layouts: none -> 20.3 us  [on_device(): qkv, out_t, fc1, fc2_t = [jnp.concatenate(list(t), axis=1) for t in flat]]
  transfers between devices with their start and end apart: 18 -> 12, of which waited for: 14 -> 10; matrix products, arithmetic and copies ran while one was open for 16% -> 17% of each run, Pallas kernels for 0% -> 16%
where the time goes in v1:
time: 974 us; the launch traced here: 966 us
  waiting for transfers between devices  377 us (39%)
  matrix products  156 us (16%)
  Pallas kernels  156 us (16%)
  local copies, waits for them, and re-layouts  112 us (11%)
  blocking collectives  111 us (11%)
  other arithmetic  29.7 us (3%)
  between operations  15.6 us (2%)
    reduce_scatter x4, waiting for transfers between devices, owned(): lax.psum_scatter(grad.astype(jnp.bfloat16), 'dp', scatter_dimension=0, ti...  226 us
    pallas_call x1, Pallas kernels, all_gather(): pl.pallas_call(ag_kernel, out_shape=shapes, in_specs=[V] * 4, out_specs=[...  156 us
    unnamed x15, waiting for transfers between devices  141 us
    unnamed x201, local copies, waits for them, and re-layouts  44.1 us
    all_gather x1, blocking collectives, on_device(): every_silu = lax.all_gather(silu_low, ('dp', 'fsdp'), axis=0, tiled=True)  43.8 us
    unnamed x1, blocking collectives  28.9 us
    another operation x3, local copies, waits for them, and re-layouts, on_device(): qkv, out_t, fc1, fc2_t = [jnp.concatenate(list(t), axis=1) for t in flat]  20.3 us
    concatenate x2, local copies, waits for them, and re-layouts, on_device(): qkv, out_t, fc1, fc2_t = [jnp.concatenate(list(t), axis=1) for t in flat]  19.6 us
  transfers between devices with their start and end apart: 12, of which 10 were waited for; matrix products, arithmetic and copies ran while one was open for 17% of the time, Pallas kernels for 16%

profile of v1, /device:TPU:0, one launch (start us, length us, event | category | flops | bytes accessed | tf_op | source)
XLA Modules:
  0.0 966.3 jit_solution(13626958406480770725)
XLA Ops:
  8.0 43.8 %all_gather.12 = bf16[32,2,1152]{2,1,0:T(2,128)(2,1)S(1)} all-gather(bf16[1,2,1152]{2,1,0:T(2,128)(2,1)S(1)} %fusion.90), channel_id=1, replica_groups=mesh['dp'=4,'fsdp'=8] {'dp','fsdp'}, dimensions={0}, use_global_device_ids=true | all-gather | bytes 152064 | tf_op jit(solution)/shard_map/all_gather | solution.py:412
  59.2 14.0 %all-gather.2 = bf16[8,1,1152]{2,1,0:T(2,128)(2,1)S(1)} all-gather(bf16[1,1,1152]{2,1,0:T(2,128)(2,1)S(1)} %reshape.1332), channel_id=2, replica_groups=mesh['dp'=4,'fsdp'=8] {'fsdp'}, dimensions={0}, use_global_device_ids=true | all-gather | bytes 20736 | tf_op jit(solution)/shard_map/all_gather | solution.py:398
  79.6 156.0 %gather_weights.1 = (bf16[4,4,2,144,864]{4,3,2,1,0:T(8,128)(2,1)S(1)}, bf16[4,4,2,144,288]{4,3,2,1,0:T(8,128)(2,1)S(1)}, bf16[4,4,2,144,1152]{4,3,2,1,0:T(8,128)(2,1)}, bf16[4,4,2,144,1152]{4,3,2,1,0:T(8,128)(2,1)}) custom-call(bf16[288,432]{1,0:T(8,128)(2,1)S(1)} %copy-done.4, bf16[144,288]{1,0:T(8,128)(2,1)S(1)} %bitcast.183, ...), custom_call_target="tpu_custom_call" | custom-call | tf_op jit(solution)/shard_map/gather_weights/pallas_call | solution.py:353
  248.7 15.1 %fusion.114 = (bf16[1,4,2,144,1152]{4,3,2,1,0:T(8,128)(2,1)}, bf16[1,4,2,144,1152]{4,3,2,1,0:T(8,128)(2,1)}, bf16[1,4,2,144,1152]{4,3,2,1,0:T(8,128)(2,1)}, bf16...) fusion(bf16[4,4,2,144,1152]{4,3,2,1,0:T(8,128)(2,1)} %get-tuple, ...), kind=kLoop, calls=%fused_computation.224 | loop fusion | bytes 42467328 | tf_op jit(solution)/shard_map/unstack | solution.py:393
  263.8 13.7 %concatenate.208 = bf16[1152,3456]{1,0:T(8,128)(2,1)} concatenate(bf16[1152,864]{1,0:T(8,128)(2,1)} %bitcast.195, bf16[1152,864]{1,0:T(8,128)(2,1)} %bitcast.194, bf16[1152,864]{1,0:T(8,128)(2,1)} %bitcast.193, bf16[1152,864]{1,0:T(8,128)(2,1)S(1)} %bitcast.192), dimensions={1} | concatenate | bytes 15925248 | tf_op jit(solution)/shard_map/concatenate | solution.py:393
  277.5 5.9 concatenate.213
  290.2 5.6 all-to-all-done
  298.2 9.3 fusion.9
  312.0 8.3 fusion.119
  334.3 14.0 %convolution_add_fusion = f32[384,4608]{1,0:T(8,128)} fusion(f32[4608]{0:T(1024)} %reshape.1304, bf16[1152,1152]{1,0:T(8,128)(2,1)} %bitcast.223, bf16[1152,1152]{1,0:T(8,128)(2,1)} %bitcast.225, bf16[1152,1152]{1,0:T(8,128)(2,1)} %bitcast.227, bf16[1152,1152]{1,0:T(8,128)(2,1)} %bitcast.221, f32[128,1152]{1,0:T(8,128)} %broadcast_in_dim.163, ...), kind=kOutput, calls=%fused_computation.16 | convolution fusion | flops 4124639232 | bytes 23024640 | tf_op jit(solution)/shard_map/itd,df->itf/dot_general | solution.py:92
  350.2 18.5 %convert_reduce_fusion = (f32[4608]{0:T(1024)}, bf16[384,4608]{1,0:T(8,128)(2,1)}) fusion(f32[384,4608]{1,0:T(8,128)} %convolution_add_fusion, bf16[1152,1152]{1,0:T(8,128)(2,1)} %bitcast.217, bf16[1152,1152]{1,0:T(8,128)(2,1)} %bitcast.215, bf16[1152,1152]{1,0:T(8,128)(2,1)} %bitcast.213, bf16[1152,1152]{1,0:T(8,128)(2,1)} %bitcast.219, ...), kind=kOutput, calls=%fused_computation.24 | convolution fusion | flops 4161351168 | bytes 23906304 | tf_op jit(solution)/shard_map/itd,fd->itf/dot_general | solution.py:448
  368.7 10.5 %fusion.73 = (f32[384]{0:T(512)S(1)}, f32[384]{0:T(512)S(1)}, f32[384,1152]{1,0:T(8,128)}) fusion(f32[128,1152]{1,0:T(8,128)} %broadcast_in_dim.163, f32[256,1152]{1,0:T(8,128)} %broadcast_in_dim.161, f32[384]{0:T(512)S(1)} %copy-done.85, f32[384,1152]{1,0:T(8,128)S(1)} %get-tuple-element.114, f32[384]{0:T(512)S(1)} %copy-done.78, ...), kind=kOutput, calls=%fused_computation.127 | convolution fusion | flops 4122868736 | bytes 19470336 | tf_op jit(solution)/shard_map/itf,df->itd/dot_general | solution.py:456
  379.3 15.8 %fusion.35 = (f32[1,384,1152]{2,1,0:T(8,128)}, bf16[1,384,1152]{2,1,0:T(8,128)(2,1)}, f32[1,384,1152]{2,1,0:T(8,128)}, f32[1152]{0:T(1024)}, f32[384,1152]{1,0:T(8,128)}) fusion(bf16[128,1152]{1,0:T(8,128)(2,1)S(1)} %bitcast.241, bf16[256,1152]{1,0:T(8,128)(2,1)} %bitcast.235, f32[384,1152]{1,0:T(8,128)S(1)} %get-tuple-element.114, ...), kind=kOutput, calls=%fused_computation.65 | convolution fusion | flops 4146756608 | bytes 33635328 | tf_op jit(solution)/shard_map/itf,fd->itd/dot_general | solution.py:96
  404.9 9.5 multiply_reduce_fusion
  414.4 10.9 %multiply_convert_fusion = bf16[16,384,384]{1,2,0:T(8,128)(2,1)} fusion(f32[16,384,384]{1,2,0:T(8,128)} %get-tuple-element.155, f32[16,384]{1,0:T(8,128)S(1)} %get-tuple-element.154, f32[16,384,384]{1,2,0:T(8,128)} %get-tuple-element.151, f32[16,384]{1,0:T(8,128)S(1)} %copy-done.67), kind=kLoop, calls=%fused_computation.10 | loop fusion | flops 9437184 | bytes 23642112 | tf_op jit(solution)/shard_map/convert_element_type | solution.py:481
  432.4 5.7 fusion.51
  440.0 7.6 convolution_convert_fusion.2
  448.8 10.8 %convolution_convert_fusion.1 = bf16[1152,4608]{1,0:T(8,128)(2,1)} fusion(bf16[384,4608]{1,0:T(8,128)(2,1)} %get-tuple-element.158, f32[128,1152]{1,0:T(8,128)} %broadcast_in_dim.163, f32[256,1152]{1,0:T(8,128)S(1)} %copy-done.37, f32[128,1152]{1,0:T(8,128)} %broadcast_in_dim.167, f32[256,1152]{1,0:T(8,128)} %broadcast_in_dim.165, ...), kind=kOutput, calls=%fused_computation.4 | convolution fusion | flops 4085710848 | bytes 19467264 | tf_op jit(solution)/shard_map/itd,itf->df/dot_general | solution.py:453
  461.4 11.6 %convolution_convert_fusion = bf16[4608,1152]{1,0:T(8,128)(2,1)} fusion(f32[128,1152]{1,0:T(8,128)S(1)} %copy-done.39, f32[256,1152]{1,0:T(8,128)S(1)} %copy-done.36, bf16[128,1152]{1,0:T(8,128)(2,1)S(1)} %bitcast.242, bf16[256,1152]{1,0:T(8,128)(2,1)S(1)} %bitcast.236, f32[384,4608]{1,0:T(8,128)} %convolution_add_fusion), kind=kOutput, calls=%fused_computation.3 | convolution fusion | flops 4101193728 | bytes 20348928 | tf_op jit(solution)/shard_map/itf,itd->fd/dot_general | solution.py:445
  474.6 8.5 fusion.74
  490.1 8.1 all_to_all.48
  498.1 7.1 all-gather.1
  508.7 19.7 %reduce-scatter.20.cloned.1.call-done = bf16[288,3456]{1,0:T(8,128)(2,1)} async-done(((bf16[1152,3456]{1,0:T(8,128)(2,1)}), bf16[288,3456]{1,0:T(8,128)(2,1)}) %reduce-scatter.20.cloned.1.call-update) | async-done | bytes 1990672 | tf_op jit(solution)/shard_map/reduce_scatter | solution.py:532
  532.8 103.6 %reduce-scatter.24.cloned.1.call-done = bf16[288,4608]{1,0:T(8,128)(2,1)} async-done(((bf16[1152,4608]{1,0:T(8,128)(2,1)}), bf16[288,4608]{1,0:T(8,128)(2,1)}) %reduce-scatter.24.cloned.1.call-update) | async-done | bytes 2654224 | tf_op jit(solution)/shard_map/reduce_scatter | solution.py:532
  641.1 103.1 %reduce-scatter.26.cloned.1.call-done = bf16[1152,1152]{1,0:T(8,128)(2,1)} async-done(((bf16[4608,1152]{1,0:T(8,128)(2,1)}), bf16[1152,1152]{1,0:T(8,128)(2,1)}) %reduce-scatter.26.cloned.1.call-update) | async-done | bytes 2654224 | tf_op jit(solution)/shard_map/reduce_scatter | solution.py:532
  744.3 5.2 copy.96
  757.4 28.9 %all-reduce.2 = f32[8,1152]{1,0:T(8,128)S(1)} all-reduce(f32[8,1152]{1,0:T(8,128)S(1)} %concatenate.235), channel_id=8, replica_groups=mesh['dp'=4,'fsdp'=8] {'fsdp'}, use_global_device_ids=true, to_apply=%region_34.35.clone | all-reduce | flops 9216 | bytes 73728
  786.9 9.2 psum.7
  809.9 24.8 %reduce-scatter.30.cloned.1.call-done = bf16[144,288]{1,0:T(8,128)(2,1)} async-done(((bf16[1152,288]{1,0:T(8,128)(2,1)}), bf16[144,288]{1,0:T(8,128)(2,1)}) %reduce-scatter.30.cloned.1.call-update) | async-done | bytes 82960
  836.5 36.5 %reduce-scatter.28.cloned.1.call-done = bf16[432,288]{1,0:T(8,128)(2,1)} async-done(((bf16[3456,288]{1,0:T(8,128)(2,1)}), bf16[432,288]{1,0:T(8,128)(2,1)}) %reduce-scatter.28.cloned.1.call-update) | async-done | bytes 248848
  875.1 43.2 %reduce-scatter.32.cloned.1.call-done = bf16[576,288]{1,0:T(8,128)(2,1)} async-done(((bf16[4608,288]{1,0:T(8,128)(2,1)}), bf16[576,288]{1,0:T(8,128)(2,1)}) %reduce-scatter.32.cloned.1.call-update) | async-done | bytes 331792
  920.5 36.2 %reduce-scatter.34.cloned.1.call-done = bf16[144,1152]{1,0:T(8,128)(2,1)} async-done(((bf16[1152,1152]{1,0:T(8,128)(2,1)}), bf16[144,1152]{1,0:T(8,128)(2,1)}) %reduce-scatter.34.cloned.1.call-update) | async-done | bytes 331792
  (356 shorter events, 129.8 us)
Async XLA Ops:
  7.2 48.7 %copy-start = (bf16[1,256,1152]{2,1,0:T(8,128)(2,1)S(1)}, bf16[1,256,1152]{2,1,0:T(8,128)(2,1)}, u32[]{:S(2)}) copy-start(bf16[1,256,1152]{2,1,0:T(8,128)(2,1)} %param.19) | copy-start | bytes 1769476
  7.2 277.0 %reduce-scatter.18.cloned.1.call-start = ((), (), s32[]{:S(2)}) async-start(), calls=%async_computation.12 | async-start | bytes 286720 | tf_op jit(solution)/shard_map/reduce_scatter | solution.py:415
  56.0 18.5 %copy-start.84 = (bf16[864]{0:T(1024)(128)(2,1)S(1)}, bf16[864]{0:T(1024)(128)(2,1)}, u32[]{:S(2)}) copy-start(bf16[864]{0:T(1024)(128)(2,1)} %param.24) | copy-start | bytes 5188
  56.9 18.9 %copy-start.22 = (bf16[128,1152]{1,0:T(8,128)(2,1)}, bf16[128,1152]{1,0:T(8,128)(2,1)S(1)}, u32[]{:S(2)}) copy-start(bf16[128,1152]{1,0:T(8,128)(2,1)S(1)} %gather_fusion) | copy-start | bytes 884740
  248.7 15.1 %copy-start.10 = (bf16[1,4,2,144,864]{4,3,2,1,0:T(8,128)(2,1)S(1)}, bf16[1,4,2,144,864]{4,3,2,1,0:T(8,128)(2,1)}, u32[]{:S(2)}) copy-start(bf16[1,4,2,144,864]{4,3,2,1,0:T(8,128)(2,1)} %get-tuple-element.123) | copy-start | bytes 5971972
  263.8 13.8 %copy-start.24 = (bf16[1,4,2,144,288]{4,3,2,1,0:T(8,128)(2,1)S(1)}, bf16[1,4,2,144,288]{4,3,2,1,0:T(8,128)(2,1)}, u32[]{:S(2)}) copy-start(bf16[1,4,2,144,288]{4,3,2,1,0:T(8,128)(2,1)} %get-tuple-element.128) | copy-start | bytes 1990660
  285.7 10.1 %all-to-all-start = ((f32[8,2,864]{2,1,0:T(2,128)}), f32[8,2,864]{2,1,0:T(2,128)S(1)}, u32[]{:S(2)}, u32[]{:S(2)}) async-start(f32[8,2,864]{2,1,0:T(2,128)} %copy.71), calls=%async_computation.1 | async-start | bytes 114688 | tf_op jit(solution)/shard_map/all_to_all | solution.py:417
  289.9 216.4 %reduce-scatter.22.cloned.1.call-start = ((), (), s32[]{:S(2)}) async-start(), calls=%async_computation.14 | async-start | bytes 3317760 | tf_op jit(solution)/shard_map/reduce_scatter | solution.py:532
  296.6 51.6 %copy-start.51 = (f32[1152]{0:T(1024)}, f32[1152]{0:T(1024)S(1)}, u32[]{:S(2)}) copy-start(f32[1152]{0:T(1024)S(1)} %get-tuple-element.104) | copy-start | bytes 13828
  296.6 52.4 %copy-start.49 = (f32[1152]{0:T(1024)}, f32[1152]{0:T(1024)S(1)}, u32[]{:S(2)}) copy-start(f32[1152]{0:T(1024)S(1)} %get-tuple-element.99) | copy-start | bytes 13828
  350.2 18.5 %copy-start.78 = (f32[384]{0:T(512)S(1)}, f32[384]{0:T(512)}, u32[]{:S(2)}) copy-start(f32[384]{0:T(512)} %copy-done.77) | copy-start | bytes 4612
  350.2 18.5 %copy-start.85 = (f32[384]{0:T(512)S(1)}, f32[384]{0:T(512)}, u32[]{:S(2)}) copy-start(f32[384]{0:T(512)} %add_rsqrt_fusion) | copy-start | bytes 4612
  368.7 10.6 %copy-start.45 = (bf16[1,128,1152]{2,1,0:T(8,128)(2,1)S(1)}, bf16[1,128,1152]{2,1,0:T(8,128)(2,1)}, u32[]{:S(2)}) copy-start(bf16[1,128,1152]{2,1,0:T(8,128)(2,1)} %param.35) | copy-start | bytes 884740
  368.7 10.6 %copy-start.80 = (f32[1152]{0:T(1024)S(1)}, f32[1152]{0:T(1024)}, u32[]{:S(2)}) copy-start(f32[1152]{0:T(1024)} %reshape.1305) | copy-start | bytes 13828
  379.3 15.9 %copy-start.8 = (bf16[1152,1152]{1,0:T(8,128)(2,1)S(1)}, bf16[1152,1152]{1,0:T(8,128)(2,1)}, u32[]{:S(2)}) copy-start(bf16[1152,1152]{1,0:T(8,128)(2,1)} %concatenate.213) | copy-start | bytes 7962628
  404.2 124.2 %reduce-scatter.20.cloned.1.call-start = ((), (), s32[]{:S(2)}) async-start(), calls=%async_computation.13 | async-start | bytes 9953280 | tf_op jit(solution)/shard_map/reduce_scatter | solution.py:532
  447.6 188.8 %reduce-scatter.24.cloned.1.call-start = ((), (), s32[]{:S(2)}) async-start(), calls=%async_computation.15 | async-start | bytes 13271040 | tf_op jit(solution)/shard_map/reduce_scatter | solution.py:532
  459.7 284.5 %reduce-scatter.26.cloned.1.call-start = ((), (), s32[]{:S(2)}) async-start(), calls=%async_computation.16 | async-start | bytes 13271040 | tf_op jit(solution)/shard_map/reduce_scatter | solution.py:532
  473.0 325.8 %all-reduce.5.cloned.1.call-start = ((), (), s32[]{:S(2)}) async-start(), calls=%async_computation.21 | async-start | bytes 196608
  474.6 8.8 copy-start.15
  474.6 8.8 copy-start.28
  474.6 8.8 copy-start.31
  488.8 16.4 %copy-start.32 = (bf16[288,864]{1,0:T(8,128)(2,1)S(1)}, bf16[288,864]{1,0:T(8,128)(2,1)}, u32[]{:S(2)}) copy-start(bf16[288,864]{1,0:T(8,128)(2,1)} %param.23) | copy-start | bytes 1492996
  506.2 328.5 %reduce-scatter.30.cloned.1.call-start = ((), (), s32[]{:S(2)}) async-start(), calls=%async_computation.18 | async-start | bytes 995328
  508.7 364.4 %reduce-scatter.28.cloned.1.call-start = ((), (), s32[]{:S(2)}) async-start(), calls=%async_computation.17 | async-start | bytes 2985984
  532.7 385.6 %reduce-scatter.32.cloned.1.call-start = ((), (), s32[]{:S(2)}) async-start(), calls=%async_computation.19 | async-start | bytes 3981312
  641.1 315.7 %reduce-scatter.34.cloned.1.call-start = ((), (), s32[]{:S(2)}) async-start(), calls=%async_computation.20 | async-start | bytes 2985984
  754.8 42.6 %copy-start.43 = (bf16[32,2,288]{2,1,0:T(2,128)(2,1)S(1)}, bf16[32,2,288]{2,1,0:T(2,128)(2,1)}, u32[]{:S(2)}) copy-start(bf16[32,2,288]{2,1,0:T(2,128)(2,1)} %copy-done.42) | copy-start | bytes 110596
  755.1 54.2 %copy-start.72 = (bf16[1,1152]{1,0:T(2,128)(2,1)S(1)}, bf16[1,1152]{1,0:T(2,128)(2,1)}, u32[]{:S(2)}) copy-start(bf16[1,1152]{1,0:T(2,128)(2,1)} %param.22) | copy-start | bytes 6916
  755.1 54.2 %copy-start.73 = (bf16[1,1152]{1,0:T(2,128)(2,1)S(1)}, bf16[1,1152]{1,0:T(2,128)(2,1)}, u32[]{:S(2)}) copy-start(bf16[1,1152]{1,0:T(2,128)(2,1)} %param.21) | copy-start | bytes 6916
  800.8 8.4 all-to-all-start.2
  918.3 40.7 %copy-start.1 = (bf16[1,256,1152]{2,1,0:T(8,128)(2,1)S(1)}, bf16[1,256,1152]{2,1,0:T(8,128)(2,1)}, u32[]{:S(2)}) copy-start(bf16[1,256,1152]{2,1,0:T(8,128)(2,1)} %param.19) | copy-start | bytes 1769476
  (73 other events, 152.8 us)
Sparse Core Ops, SparseCore 0:
  54.7 19.4 reduce-scatter.17
  404.3 37.2 reduce-scatter.21
  447.7 80.6 reduce-scatter.19
  531.7 104.6 reduce-scatter.23
  639.6 104.6 reduce-scatter.25
  747.1 51.6 all-reduce.4
  801.1 33.5 reduce-scatter.29
  837.1 35.8 reduce-scatter.27
  875.5 42.7 reduce-scatter.31
  920.4 36.2 reduce-scatter.33
